TPU v7x, 32 devices: a whole 2x2x4 slice. The times are simulated.
32 devices in a mesh: slab: 8 (over z, y), grp: 4 (over x, core).
Axes of the slice: x: 2, y: 2, z: 4, core: 2. Of those that a mesh axis runs over, the one named last changes fastest.
Arguments:
- positions: float32 [32, 16, 3, 128], P('slab', 'grp'), may hold values from 0 to 1
- sketch: bfloat16 [32, 16, 128, 256], P('slab', 'grp'), may hold values from -6 to 6
- counts: int32 [32, 16], P('slab', 'grp'), may hold values from 32 to 128, as said below
- neighbours: int32 [32, 16, 8], P('slab', 'grp'), may hold values from 0 to 8, as said below
Outputs:
- basis: bfloat16 [32, 16, 128, 256], P('slab', 'grp')
- factor: float32 [256, 256], replicated
Inputs may be any that keep to these rules, and one draw needn't show every extreme that they name: `counts`: the first block of every device's region of 4 x 4 blocks is full. `neighbours`: a code is 3 (dz + 1) + (dy + 1) for offsets dz, dy in -1, 0, 1; the codes of one block are distinct and always include 4 (the block itself); each block leaves out exactly one of its nine codes, and the lists are symmetric: block a lists block b if and only if block b lists block a; the left-out pairs lie inside aligned 2 x 2 squares of blocks.
All inputs are finite; a program needn't handle non-finite values.
Results may differ from a plain program's by a relative error of at most 0.017.
Values may be sent and summed in bfloat16 or wider, within the bound.
A program may use at most 64 MiB of HBM per device.

v0:
```python
import math
import jax
import jax.numpy as jnp
from jax import lax
from jax.sharding import PartitionSpec as P


def padded(shard, sides, width):
    for axis, dim in sides:
        count, length = (lax.axis_size(axis), shard.shape[dim])
        up = [(i, (i + 1) % count) for i in range(count)]
        down = [(j, i) for i, j in up]
        last = lax.slice_in_dim(shard, length - width, length, axis=dim)
        leading = lax.slice_in_dim(shard, 0, width, axis=dim)
        before = lax.ppermute(last, axis, up)
        after = lax.ppermute(leading, axis, down)
        shard = jnp.concatenate([before, shard, after], axis=dim)
    return shard


def kernel_tile(own_pos, other_pos, shift_z, shift_y):
    diff_z = other_pos[..., 0, None, :] + shift_z[..., None, None] - own_pos[..., 0, :, None]
    diff_y = other_pos[..., 1, None, :] + shift_y[..., None, None] - own_pos[..., 1, :, None]
    diff_x = other_pos[..., 2, None, :] - own_pos[..., 2, :, None]
    radius = jnp.sqrt(diff_z * diff_z + diff_y * diff_y + diff_x * diff_x)
    taper = jnp.maximum(1.0 - radius, 0.0)
    return taper**4 * (4.0 * radius + 1.0)


def on_device(positions, sketch, counts, neighbours):
    blocks_z, blocks_y, _, points = positions.shape
    columns = sketch.shape[3]
    live_mask = (
        lax.broadcasted_iota(jnp.int32, (blocks_z, blocks_y, points), 2) < counts[:, :, None]
    )
    masked = jnp.where(live_mask[..., None], sketch, jnp.zeros_like(sketch))
    wide_pos, wide_rows = (
        padded(positions.astype(jnp.bfloat16), (("slab", 0), ("grp", 1)), 1).astype(
            positions.dtype
        ),
        padded(masked, (("slab", 0), ("grp", 1)), 1),
    )
    pos_table = wide_pos.reshape(-1, 3, points)
    row_table = wide_rows.reshape(-1, points, columns)
    own_pos = positions.reshape(-1, 3, points)
    row_ids = lax.broadcasted_iota(jnp.int32, (blocks_z, blocks_y), 0)
    col_ids = lax.broadcasted_iota(jnp.int32, (blocks_z, blocks_y), 1)
    image = jnp.zeros((blocks_z * blocks_y, points, columns), jnp.float32)
    for slot_index in range(neighbours.shape[2]):
        offset_code = neighbours[:, :, slot_index]
        shift_z = offset_code // 3 - 1
        shift_y = offset_code % 3 - 1
        source_ids = ((row_ids + 1 + shift_z) * (blocks_y + 2) + col_ids + 1 + shift_y).reshape(-1)
        other_pos = jnp.take(pos_table, source_ids, axis=0)
        other_rows = jnp.take(row_table, source_ids, axis=0)
        weights = kernel_tile(
            own_pos,
            other_pos,
            shift_z.reshape(-1).astype(jnp.float32),
            shift_y.reshape(-1).astype(jnp.float32),
        ).astype(jnp.bfloat16)
        image = image + jnp.einsum(
            "bij,bjr->bir", weights, other_rows, preferred_element_type=jnp.float32
        )
    image = jnp.where(live_mask.reshape(-1, points)[..., None], image, jnp.zeros_like(image))
    flat_rows = image.reshape(-1, columns)
    gram_local = jnp.dot(
        flat_rows.T, flat_rows, preferred_element_type=jnp.float32, precision=lax.Precision.HIGHEST
    )
    gram_total = lax.psum(gram_local, ("slab", "grp"))
    lower_factor = jnp.linalg.cholesky(gram_total)
    solved = lax.linalg.triangular_solve(lower_factor, flat_rows.T, left_side=True, lower=True)
    total_rows = lax.axis_size("slab") * blocks_z * lax.axis_size("grp") * blocks_y * points
    scale_rows = math.sqrt(total_rows)
    basis = (
        (solved.T * scale_rows).reshape(blocks_z, blocks_y, points, columns).astype(jnp.bfloat16)
    )
    factor = lower_factor.T / scale_rows
    return (basis, factor)


def solution(mesh):
    placed = (
        P("slab", "grp", None, None),
        P("slab", "grp", None, None),
        P("slab", "grp"),
        P("slab", "grp", None),
    )
    return jax.shard_map(
        on_device,
        mesh=mesh,
        in_specs=placed,
        out_specs=(P("slab", "grp", None, None), P()),
        check_vma=False,
    )
```

profile of v0, /device:TPU:0, one launch (start us, length us, event | category | flops | bytes accessed | tf_op | source)
XLA Modules:
  0.0 279.9 jit_solution(16708323109046703102)
XLA Ops:
  7.2 0.7 convert_element_type.155
  8.0 3.0 %collective-permute-start = (bf16[1,4,3,128]{3,1,2,0:T(4,128)(2,1)S(1)}, bf16[1,4,3,128]{3,1,2,0:T(4,128)(2,1)S(1)}, u32[]{:S(2)}, u32[]{:S(2)}) collective-permute-start(bf16[1,4,3,128]{3,1,2,0:T(4,128)(2,1)S(1)} %get-tuple-element.121), channel_id=1, source_target_pairs={{0,4},{4,8},{8,12},{12,16},{16,20},{20,24},{24,28},{28,0},{1,5},{5... | collective-permute-start | bytes 9224 | tf_op jit(solution)/shard_map/ppermute | solution.py:15
  11.0 3.1 %collective-permute-start.1 = (bf16[1,4,3,128]{3,1,2,0:T(4,128)(2,1)S(1)}, bf16[1,4,3,128]{3,1,2,0:T(4,128)(2,1)S(1)}, u32[]{:S(2)}, u32[]{:S(2)}) collective-permute-start(bf16[1,4,3,128]{3,1,2,0:T(4,128)(2,1)S(1)} %get-tuple-element.122), channel_id=1, source_target_pairs={{4,0},{8,4},{12,8},{16,12},{20,16},{24,20},{28,24},{0,28},{5,1},{9... | collective-permute-start | bytes 9224 | tf_op jit(solution)/shard_map/ppermute | solution.py:16
  14.1 0.8 iota_compare_fusion.3
  14.9 1.5 broadcast_select_fusion
  16.5 4.7 %collective-permute-start.5 = (bf16[1,4,128,256]{3,2,1,0:T(8,128)(2,1)S(1)}, bf16[1,4,128,256]{3,2,1,0:T(8,128)(2,1)S(1)}, u32[]{:S(2)}, u32[]{:S(2)}) collective-permute-start(bf16[1,4,128,256]{3,2,1,0:T(8,128)(2,1)S(1)} %get-tuple-element.85), channel_id=1, source_target_pairs={{4,0},{8,4},{12,8},{16,12},{20,16},{24,20},{28,24},{0,28},{5,1},{9... | collective-permute-start | bytes 786440 | tf_op jit(solution)/shard_map/ppermute | solution.py:16
  21.3 0.7 fusion.121
  22.0 1.3 remainder_reduce_fusion
  26.2 1.7 collective-permute-start.3
  28.0 1.3 collective-permute-done.2
  34.4 0.7 slice_add_fusion.11
  36.6 1.7 collective-permute-start.6
  39.2 0.7 slice_add_fusion.15
  39.9 6.3 %collective-permute-done.6 = bf16[6,1,128,256]{3,2,1,0:T(8,128)(2,1)S(1)} collective-permute-done((bf16[6,1,128,256]{3,2,1,0:T(8,128)(2,1)S(1)}, bf16[6,1,128,256]{3,2,1,0:T(8,128)(2,1)S(1)}, u32[]{:S(2)}, u32[]{:S(2)}) %collective-permute-start.6) | collective-permute-done | bytes 393248 | tf_op jit(solution)/shard_map/ppermute | solution.py:15
  46.2 1.0 collective-permute-done.7
  47.2 1.4 pad_maximum_fusion
  49.2 1.7 gather_fusion.13
  50.9 1.7 gather_fusion.11
  52.6 1.7 gather_fusion.9
  54.3 1.7 gather_fusion.7
  56.0 1.7 gather_fusion.5
  57.8 1.8 gather_fusion.3
  59.6 1.8 gather_fusion.1
  61.4 2.4 fusion.5
  63.9 1.7 fusion.7
  65.6 1.7 fusion.9
  67.4 1.7 fusion.11
  69.2 1.7 fusion.13
  71.0 1.7 fusion.17
  72.7 1.7 fusion.15
  74.5 2.8 add_select_fusion
  77.2 4.2 %convolution_bitcast_fusion = f32[256,256]{0,1:T(8,128)} fusion(f32[16,128,256]{2,1,0:T(8,128)S(1)} %add_select_fusion), kind=kOutput, calls=%fused_computation.23 | convolution fusion | flops 1610612736 | bytes 2359296 | tf_op jit(solution)/shard_map/dot_general | solution.py:67
  81.4 122.8 %all-reduce.3.cloned.1.call-done = f32[256,256]{0,1:T(8,128)} async-done(((f32[256,256]{0,1:T(8,128)}), f32[256,256]{0,1:T(8,128)}) %all-reduce.3.cloned.1.call-update) | async-done | bytes 262160 | tf_op jit(solution)/shard_map/psum | solution.py:70
  204.2 1.1 copy.23
  205.3 1.0 fusion.107
  206.3 11.7 %cholesky.50 = f32[128,128]{1,0:T(8,128)S(1)} custom-call(f32[128,128]{1,0:T(8,128)S(1)} %cholesky.118), custom_call_target="Cholesky" | custom-call | tf_op jit(solution)/shard_map/jit(cholesky)/cholesky | solution.py:71
  218.7 9.8 %custom-call.14 = f32[1,128,128]{1,2,0:T(8,128)S(1)} custom-call(f32[1,128,128]{2,1,0:T(8,128)S(1)} %get-tuple-element.91), custom_call_target="InvertDiagBlocksLowerTriangular" | custom-call | tf_op jit(solution)/shard_map/jit(cholesky)/cholesky | solution.py:71
  229.0 11.9 %cholesky.105 = f32[128,128]{1,0:T(8,128)S(1)} custom-call(f32[128,128]{1,0:T(8,128)S(1)} %convolution_subtract_fusion.1), custom_call_target="Cholesky" | custom-call | tf_op jit(solution)/shard_map/jit(cholesky)/cholesky | solution.py:71
  241.0 0.7 compare_reduce_fusion
  243.0 0.8 copy.25
  243.9 4.0 %while.1 = (s32[]{:T(128)}, f32[256,256]{1,0:T(8,128)S(1)}, s32[2,2]{1,0:T(2,128)S(1)}, f32[2,128,128]{2,1,0:T(8,128)S(1)}, s32[]{:T(128)}) while((s32[]{:T(128)}, f32[256,256]{1,0:T(8,128)S(1)}, s32[2,2]{1,0:T(2,128)S(1)}, f32[2,128,128]{2,1,0:T(8,128)S(1)}, s32[]{:T(128)}) %tuple.117), condition=%wide.while_cond, body=%wide.while_body.sunk | while | flops 2 | bytes 131189 | solution.py:72
  244.6 1.3 bitcast_dynamic-update-slice_fusion.2
  246.6 1.3 bitcast_dynamic-update-slice_fusion.2
  247.9 19.7 %custom-call.15 = f32[2,128,128]{1,2,0:T(8,128)S(1)} custom-call(f32[2,128,128]{2,1,0:T(8,128)S(1)} %get-tuple-element.11), custom_call_target="InvertDiagBlocksLowerTriangular" | custom-call | tf_op jit(solution)/shard_map/triangular_solve | solution.py:72
  267.6 1.1 fusion.2
  268.7 1.8 convolution_subtract_fusion
  270.5 1.1 fusion.110
  271.8 1.3 copy.29
  (190 shorter events, 13.7 us)
Async XLA Ops:
  7.2 14.1 %copy-start.9 = (f32[4,4,3,128]{3,1,2,0:T(4,128)S(1)}, f32[4,4,3,128]{3,1,2,0:T(4,128)}, u32[]{:S(2)}) copy-start(f32[4,4,3,128]{3,1,2,0:T(4,128)} %param.8) | copy-start | bytes 73732
  7.2 14.0 %copy-start.20 = (s32[4,4]{1,0:T(4,128)S(1)}, s32[4,4]{1,0:T(4,128)}, u32[]{:S(2)}) copy-start(s32[4,4]{1,0:T(4,128)} %param.10) | copy-start | bytes 196
  7.2 14.1 %copy-start = (s32[4,4,8]{2,1,0:T(4,128)S(1)}, s32[4,4,8]{2,1,0:T(4,128)}, u32[]{:S(2)}) copy-start(s32[4,4,8]{2,1,0:T(4,128)} %param.11) | copy-start | bytes 1540
  7.2 197.0 %all-reduce.3.cloned.1.call-start = ((), (), s32[]{:S(2)}) async-start(), calls=%async_computation | async-start | bytes 524288 | tf_op jit(solution)/shard_map/psum | solution.py:70
  8.0 18.1 %collective-permute-start = (bf16[1,4,3,128]{3,1,2,0:T(4,128)(2,1)S(1)}, bf16[1,4,3,128]{3,1,2,0:T(4,128)(2,1)S(1)}, u32[]{:S(2)}, u32[]{:S(2)}) collective-permute-start(bf16[1,4,3,128]{3,1,2,0:T(4,128)(2,1)S(1)} %get-tuple-element.121), channel_id=1, source_target_pairs={{0,4},{4,8},{8,12},{12,16},{16,20},{20,24},{24,28},{28,0},{1,5},{5... | collective-permute-start | bytes 9224 | tf_op jit(solution)/shard_map/ppermute | solution.py:15
  11.0 15.1 %collective-permute-start.1 = (bf16[1,4,3,128]{3,1,2,0:T(4,128)(2,1)S(1)}, bf16[1,4,3,128]{3,1,2,0:T(4,128)(2,1)S(1)}, u32[]{:S(2)}, u32[]{:S(2)}) collective-permute-start(bf16[1,4,3,128]{3,1,2,0:T(4,128)(2,1)S(1)} %get-tuple-element.122), channel_id=1, source_target_pairs={{4,0},{8,4},{12,8},{16,12},{20,16},{24,20},{28,24},{0,28},{5,1},{9... | collective-permute-start | bytes 9224 | tf_op jit(solution)/shard_map/ppermute | solution.py:16
  16.4 20.1 %collective-permute-start.4 = (bf16[1,4,128,256]{3,2,1,0:T(8,128)(2,1)S(1)}, bf16[1,4,128,256]{3,2,1,0:T(8,128)(2,1)S(1)}, u32[]{:S(2)}, u32[]{:S(2)}) collective-permute-start(bf16[1,4,128,256]{3,2,1,0:T(8,128)(2,1)S(1)} %get-tuple-element.84), channel_id=1, source_target_pairs={{0,4},{4,8},{8,12},{12,16},{16,20},{20,24},{24,28},{28,0},{1,5},{5... | collective-permute-start | bytes 786440 | tf_op jit(solution)/shard_map/ppermute | solution.py:15
  16.5 20.0 %collective-permute-start.5 = (bf16[1,4,128,256]{3,2,1,0:T(8,128)(2,1)S(1)}, bf16[1,4,128,256]{3,2,1,0:T(8,128)(2,1)S(1)}, u32[]{:S(2)}, u32[]{:S(2)}) collective-permute-start(bf16[1,4,128,256]{3,2,1,0:T(8,128)(2,1)S(1)} %get-tuple-element.85), channel_id=1, source_target_pairs={{4,0},{8,4},{12,8},{16,12},{20,16},{24,20},{28,24},{0,28},{5,1},{9... | collective-permute-start | bytes 786440 | tf_op jit(solution)/shard_map/ppermute | solution.py:16
  25.8 7.3 %copy-start.28 = (pred[16]{0:T(512)(128)(4,1)}, pred[16]{0:T(512)(128)(4,1)S(1)}, u32[]{:S(2)}) copy-start(pred[16]{0:T(512)(128)(4,1)S(1)} %get-tuple-element.50) | copy-start | bytes 52
  25.9 7.9 %copy-start.34 = (pred[16]{0:T(512)(128)(4,1)}, pred[16]{0:T(512)(128)(4,1)S(1)}, u32[]{:S(2)}) copy-start(pred[16]{0:T(512)(128)(4,1)S(1)} %get-tuple-element.131) | copy-start | bytes 52
  25.9 7.9 %copy-start.36 = (pred[16]{0:T(512)(128)(4,1)}, pred[16]{0:T(512)(128)(4,1)S(1)}, u32[]{:S(2)}) copy-start(pred[16]{0:T(512)(128)(4,1)S(1)} %get-tuple-element.129) | copy-start | bytes 52
  25.9 7.9 %copy-start.38 = (pred[16]{0:T(512)(128)(4,1)}, pred[16]{0:T(512)(128)(4,1)S(1)}, u32[]{:S(2)}) copy-start(pred[16]{0:T(512)(128)(4,1)S(1)} %get-tuple-element.127) | copy-start | bytes 52
  25.9 7.9 %copy-start.40 = (pred[16]{0:T(512)(128)(4,1)}, pred[16]{0:T(512)(128)(4,1)S(1)}, u32[]{:S(2)}) copy-start(pred[16]{0:T(512)(128)(4,1)S(1)} %get-tuple-element.125) | copy-start | bytes 52
  25.9 10.4 %copy-start.42 = (pred[16]{0:T(512)(128)(4,1)}, pred[16]{0:T(512)(128)(4,1)S(1)}, u32[]{:S(2)}) copy-start(pred[16]{0:T(512)(128)(4,1)S(1)} %get-tuple-element.123) | copy-start | bytes 52
  25.9 13.3 %copy-start.30 = (pred[16]{0:T(512)(128)(4,1)}, pred[16]{0:T(512)(128)(4,1)S(1)}, u32[]{:S(2)}) copy-start(pred[16]{0:T(512)(128)(4,1)S(1)} %get-tuple-element.133) | copy-start | bytes 52
  25.9 13.3 %copy-start.32 = (pred[16]{0:T(512)(128)(4,1)}, pred[16]{0:T(512)(128)(4,1)S(1)}, u32[]{:S(2)}) copy-start(pred[16]{0:T(512)(128)(4,1)S(1)} %get-tuple-element.135) | copy-start | bytes 52
  25.9 7.1 %copy-start.21 = (s32[1024]{0:T(1024)}, s32[1024]{0:T(1024)S(1)}, u32[]{:S(2)}) copy-start(s32[1024]{0:T(1024)S(1)} %pad_clamp_fusion.1) | copy-start | bytes 12292
  26.0 7.1 %copy-start.22 = (s32[1024]{0:T(1024)}, s32[1024]{0:T(1024)S(1)}, u32[]{:S(2)}) copy-start(s32[1024]{0:T(1024)S(1)} %pad_clamp_fusion.2) | copy-start | bytes 12292
  26.0 7.2 %copy-start.23 = (s32[1024]{0:T(1024)}, s32[1024]{0:T(1024)S(1)}, u32[]{:S(2)}) copy-start(s32[1024]{0:T(1024)S(1)} %pad_clamp_fusion.3) | copy-start | bytes 12292
  26.0 7.1 %copy-start.24 = (s32[1024]{0:T(1024)}, s32[1024]{0:T(1024)S(1)}, u32[]{:S(2)}) copy-start(s32[1024]{0:T(1024)S(1)} %pad_clamp_fusion.4) | copy-start | bytes 12292
  26.0 7.1 %copy-start.25 = (s32[1024]{0:T(1024)}, s32[1024]{0:T(1024)S(1)}, u32[]{:S(2)}) copy-start(s32[1024]{0:T(1024)S(1)} %pad_clamp_fusion.5) | copy-start | bytes 12292
  26.1 10.3 %copy-start.26 = (s32[1024]{0:T(1024)}, s32[1024]{0:T(1024)S(1)}, u32[]{:S(2)}) copy-start(s32[1024]{0:T(1024)S(1)} %pad_clamp_fusion.6) | copy-start | bytes 12292
  26.2 3.1 %collective-permute-start.2 = (bf16[6,1,3,128]{3,1,2,0:T(2,128)(2,1)S(1)}, bf16[6,1,3,128]{3,1,2,0:T(2,128)(2,1)S(1)}, u32[]{:S(2)}, u32[]{:S(2)}) collective-permute-start(bf16[6,1,3,128]{3,1,2,0:T(2,128)(2,1)S(1)} %get-tuple-element.119), channel_id=1, source_target_pairs={{0,1},{1,2},{2,3},{3,0},{4,5},{5,6},{6,7},{7,4},{8,9},{9,10},{10,1... | collective-permute-start | bytes 13832 | tf_op jit(solution)/shard_map/ppermute | solution.py:15
  26.2 3.1 %collective-permute-start.3 = (bf16[6,1,3,128]{3,1,2,0:T(2,128)(2,1)S(1)}, bf16[6,1,3,128]{3,1,2,0:T(2,128)(2,1)S(1)}, u32[]{:S(2)}, u32[]{:S(2)}) collective-permute-start(bf16[6,1,3,128]{3,1,2,0:T(2,128)(2,1)S(1)} %get-tuple-element.120), channel_id=1, source_target_pairs={{1,0},{2,1},{3,2},{0,3},{5,4},{6,5},{7,6},{4,7},{9,8},{10,9},{11,1... | collective-permute-start | bytes 13832 | tf_op jit(solution)/shard_map/ppermute | solution.py:16
  28.0 8.4 %copy-start.27 = (s32[1024]{0:T(1024)}, s32[1024]{0:T(1024)S(1)}, u32[]{:S(2)}) copy-start(s32[1024]{0:T(1024)S(1)} %pad_clamp_fusion.7) | copy-start | bytes 12292
  36.5 9.7 %copy-start.1 = (bf16[1,4,128,256]{3,2,1,0:T(8,128)(2,1)}, bf16[1,4,128,256]{3,2,1,0:T(8,128)(2,1)S(1)}, u32[]{:S(2)}) copy-start(bf16[1,4,128,256]{3,2,1,0:T(8,128)(2,1)S(1)} %collective-permute-done.4) | copy-start | bytes 786436
  36.5 9.7 %copy-start.2 = (bf16[1,4,128,256]{3,2,1,0:T(8,128)(2,1)}, bf16[1,4,128,256]{3,2,1,0:T(8,128)(2,1)S(1)}, u32[]{:S(2)}) copy-start(bf16[1,4,128,256]{3,2,1,0:T(8,128)(2,1)S(1)} %collective-permute-done.5) | copy-start | bytes 786436
  36.6 9.6 %collective-permute-start.6 = (bf16[6,1,128,256]{3,2,1,0:T(8,128)(2,1)S(1)}, bf16[6,1,128,256]{3,2,1,0:T(8,128)(2,1)S(1)}, u32[]{:S(2)}, u32[]{:S(2)}) collective-permute-start(bf16[6,1,128,256]{3,2,1,0:T(8,128)(2,1)S(1)} %get-tuple-element.82), channel_id=1, source_target_pairs={{0,1},{1,2},{2,3},{3,0},{4,5},{5,6},{6,7},{7,4},{8,9},{9,10},{10,1... | collective-permute-start | bytes 1179656 | tf_op jit(solution)/shard_map/ppermute | solution.py:15
  38.3 8.9 %collective-permute-start.7 = (bf16[6,1,128,256]{3,2,1,0:T(8,128)(2,1)S(1)}, bf16[6,1,128,256]{3,2,1,0:T(8,128)(2,1)S(1)}, u32[]{:S(2)}, u32[]{:S(2)}) collective-permute-start(bf16[6,1,128,256]{3,2,1,0:T(8,128)(2,1)S(1)} %get-tuple-element.83), channel_id=1, source_target_pairs={{1,0},{2,1},{3,2},{0,3},{5,4},{6,5},{7,6},{4,7},{9,8},{10,9},{11,1... | collective-permute-start | bytes 1179656 | tf_op jit(solution)/shard_map/ppermute | solution.py:16
  57.8 3.6 %copy-start.43 = (pred[16]{0:T(512)(128)(4,1)S(1)}, pred[16]{0:T(512)(128)(4,1)}, u32[]{:S(2)}) copy-start(pred[16]{0:T(512)(128)(4,1)} %copy-done.42) | copy-start | bytes 52
  61.4 2.4 copy-start.8
  61.4 2.4 copy-start.41
  65.6 1.7 copy-start.6
  67.3 1.8 copy-start.5
  67.3 1.8 copy-start.11
  67.4 1.8 copy-start.12
  67.4 1.8 copy-start.13
  67.4 1.8 copy-start.35
  69.1 1.8 copy-start.4
  69.1 1.8 copy-start.17
  69.2 1.8 copy-start.18
  69.2 1.8 copy-start.19
  69.2 1.8 copy-start.33
  70.9 1.8 copy-start.3
  70.9 1.8 copy-start.14
  71.0 1.8 copy-start.15
  71.0 1.8 copy-start.16
  71.0 1.8 copy-start.31
  (5 other events, 8.6 us)
Sparse Core Ops, SparseCore 0:
  81.5 122.6 all-reduce.2
where the time goes:
time: 280 us
  waiting for transfers between devices  131 us (47%)
  other arithmetic  66.1 us (24%)
  local copies, waits for them, and re-layouts  27.4 us (10%)
  matrix products  24 us (9%)
  between operations  16.4 us (6%)
  starting transfers between devices  14.6 us (5%)
    psum x1, waiting for transfers between devices, on_device(): gram_total = lax.psum(gram_local, ('slab', 'grp'))  123 us
    another operation x7, other arithmetic, on_device(): lower_factor = jnp.linalg.cholesky(gram_total)  34.8 us
    another operation x2, other arithmetic, on_device(): lax.linalg.triangular_solve(lower_factor, flat_rows.T, left_side=True, lo...  19.7 us
    dot_general x8, matrix products, on_device(): jnp.einsum('bij,bjr->bir', weights, other_rows, preferred_element_type=jn...  15.4 us
    gather x8, local copies, waits for them, and re-layouts, on_device(): other_rows = jnp.take(row_table, source_ids, axis=0)  12.8 us
    ppermute x4, starting transfers between devices, padded(): after = lax.ppermute(leading, axis, down)  9.73 us
    ppermute x4, waiting for transfers between devices, padded(): before = lax.ppermute(last, axis, up)  7.6 us
  transfers between devices with their start and end apart: 9, of which 4 were waited for; matrix products, arithmetic and copies ran while one was open for 5% of the time, Pallas kernels for 0%

commit v1 on v0

--- a/solution.py
+++ b/solution.py
@@ -67,7 +67,8 @@
     gram_local = jnp.dot(
         flat_rows.T, flat_rows, preferred_element_type=jnp.float32, precision=lax.Precision.HIGHEST
     )
-    gram_total = lax.psum(gram_local, ("slab", "grp"))
+    one_axis = lax.psum(gram_local, "grp")
+    gram_total = lax.psum(one_axis, "slab")
     lower_factor = jnp.linalg.cholesky(gram_total)
     solved = lax.linalg.triangular_solve(lower_factor, flat_rows.T, left_side=True, lower=True)
     total_rows = lax.axis_size("slab") * blocks_z * lax.axis_size("grp") * blocks_y * points

time: 280 us -> 261 us (0.932)
  waiting for transfers between devices: 131 us -> 112 us
    psum x1 -> x2, waiting for transfers between devices: 123 us -> 104 us  [the longest x1 74.2 us: on_device(): gram_total = lax.psum(one_axis, 'slab')]
  transfers between devices with their start and end apart: 9 -> 10, of which waited for: 4 -> 5; matrix products, arithmetic and copies ran while one was open for 5% -> 6% of each run, Pallas kernels for 0% -> 0%
where the time goes in v1:
time: 261 us
  waiting for transfers between devices  112 us (43%)
  other arithmetic  65.9 us (25%)
  local copies, waits for them, and re-layouts  27.4 us (10%)
  matrix products  23.8 us (9%)
  between operations  16.4 us (6%)
  starting transfers between devices  15.1 us (6%)
    psum x1, waiting for transfers between devices, on_device(): gram_total = lax.psum(one_axis, 'slab')  74.2 us
    another operation x7, other arithmetic, on_device(): lower_factor = jnp.linalg.cholesky(gram_total)  34.6 us
    psum x1, waiting for transfers between devices, on_device(): one_axis = lax.psum(gram_local, 'grp')  29.6 us
    another operation x2, other arithmetic, on_device(): lax.linalg.triangular_solve(lower_factor, flat_rows.T, left_side=True, lo...  19.7 us
    dot_general x8, matrix products, on_device(): jnp.einsum('bij,bjr->bir', weights, other_rows, preferred_element_type=jn...  15.2 us
    gather x8, local copies, waits for them, and re-layouts, on_device(): other_rows = jnp.take(row_table, source_ids, axis=0)  12.8 us
    ppermute x4, starting transfers between devices, padded(): after = lax.ppermute(leading, axis, down)  9.91 us
    ppermute x4, waiting for transfers between devices, padded(): before = lax.ppermute(last, axis, up)  7.23 us
  transfers between devices with their start and end apart: 10, of which 5 were waited for; matrix products, arithmetic and copies ran while one was open for 6% of the time, Pallas kernels for 0%

profile of v1, /device:TPU:0, one launch (start us, length us, event | category | flops | bytes accessed | tf_op | source)
XLA Modules:
  0.0 260.8 jit_solution(10731194955963154727)
XLA Ops:
  7.2 0.7 convert_element_type.155
  8.0 3.0 %collective-permute-start = (bf16[1,4,3,128]{3,1,2,0:T(4,128)(2,1)S(1)}, bf16[1,4,3,128]{3,1,2,0:T(4,128)(2,1)S(1)}, u32[]{:S(2)}, u32[]{:S(2)}) collective-permute-start(bf16[1,4,3,128]{3,1,2,0:T(4,128)(2,1)S(1)} %get-tuple-element.121), channel_id=1, source_target_pairs={{0,4},{4,8},{8,12},{12,16},{16,20},{20,24},{24,28},{28,0},{1,5},{5... | collective-permute-start | bytes 9224 | tf_op jit(solution)/shard_map/ppermute | solution.py:15
  11.0 3.1 %collective-permute-start.1 = (bf16[1,4,3,128]{3,1,2,0:T(4,128)(2,1)S(1)}, bf16[1,4,3,128]{3,1,2,0:T(4,128)(2,1)S(1)}, u32[]{:S(2)}, u32[]{:S(2)}) collective-permute-start(bf16[1,4,3,128]{3,1,2,0:T(4,128)(2,1)S(1)} %get-tuple-element.122), channel_id=1, source_target_pairs={{4,0},{8,4},{12,8},{16,12},{20,16},{24,20},{28,24},{0,28},{5,1},{9... | collective-permute-start | bytes 9224 | tf_op jit(solution)/shard_map/ppermute | solution.py:16
  14.1 0.8 iota_compare_fusion.3
  14.9 1.5 broadcast_select_fusion
  16.5 4.7 %collective-permute-start.5 = (bf16[1,4,128,256]{3,2,1,0:T(8,128)(2,1)S(1)}, bf16[1,4,128,256]{3,2,1,0:T(8,128)(2,1)S(1)}, u32[]{:S(2)}, u32[]{:S(2)}) collective-permute-start(bf16[1,4,128,256]{3,2,1,0:T(8,128)(2,1)S(1)} %get-tuple-element.85), channel_id=1, source_target_pairs={{4,0},{8,4},{12,8},{16,12},{20,16},{24,20},{28,24},{0,28},{5,1},{9... | collective-permute-start | bytes 786440 | tf_op jit(solution)/shard_map/ppermute | solution.py:16
  21.3 0.7 fusion.121
  22.0 1.3 remainder_reduce_fusion
  26.2 1.7 collective-permute-start.3
  28.0 1.3 collective-permute-done.2
  34.4 0.7 slice_add_fusion.11
  36.6 1.7 collective-permute-start.6
  39.4 0.7 slice_add_fusion.15
  40.1 5.9 %collective-permute-done.6 = bf16[6,1,128,256]{3,2,1,0:T(8,128)(2,1)S(1)} collective-permute-done((bf16[6,1,128,256]{3,2,1,0:T(8,128)(2,1)S(1)}, bf16[6,1,128,256]{3,2,1,0:T(8,128)(2,1)S(1)}, u32[]{:S(2)}, u32[]{:S(2)}) %collective-permute-start.6) | collective-permute-done | bytes 393248 | tf_op jit(solution)/shard_map/ppermute | solution.py:15
  46.0 1.2 collective-permute-done.7
  47.2 1.4 pad_maximum_fusion
  49.2 1.7 gather_fusion.13
  50.9 1.7 gather_fusion.11
  52.6 1.7 gather_fusion.9
  54.3 1.7 gather_fusion.7
  56.0 1.7 gather_fusion.5
  57.8 1.8 gather_fusion.3
  59.6 1.8 gather_fusion.1
  61.4 2.4 fusion.5
  63.8 1.7 fusion.7
  65.6 1.7 fusion.9
  67.4 1.7 fusion.11
  69.2 1.7 fusion.13
  71.0 1.7 fusion.17
  72.7 1.7 fusion.15
  74.4 2.6 add_select_fusion
  77.0 4.2 %convolution_bitcast_fusion = f32[256,256]{0,1:T(8,128)} fusion(f32[16,128,256]{2,1,0:T(8,128)S(1)} %add_select_fusion), kind=kOutput, calls=%fused_computation.23 | convolution fusion | flops 1610612736 | bytes 2359296 | tf_op jit(solution)/shard_map/dot_general | solution.py:67
  81.5 29.6 %all-reduce.4.cloned.1.call-done = f32[256,256]{0,1:T(8,128)} async-done(((f32[256,256]{0,1:T(8,128)}), f32[256,256]{0,1:T(8,128)}) %all-reduce.4.cloned.1.call-update) | async-done | bytes 262160 | tf_op jit(solution)/shard_map/psum | solution.py:70
  111.1 74.2 %all-reduce.6.cloned.1.call-done = f32[256,256]{0,1:T(8,128)} async-done(((f32[256,256]{0,1:T(8,128)}), f32[256,256]{0,1:T(8,128)}) %all-reduce.6.cloned.1.call-update) | async-done | bytes 262160 | tf_op jit(solution)/shard_map/psum | solution.py:71
  185.4 1.1 copy.23
  186.4 1.0 fusion.107
  187.4 11.7 %cholesky.50 = f32[128,128]{1,0:T(8,128)S(1)} custom-call(f32[128,128]{1,0:T(8,128)S(1)} %cholesky.118), custom_call_target="Cholesky" | custom-call | tf_op jit(solution)/shard_map/jit(cholesky)/cholesky | solution.py:72
  199.8 9.8 %custom-call.14 = f32[1,128,128]{1,2,0:T(8,128)S(1)} custom-call(f32[1,128,128]{2,1,0:T(8,128)S(1)} %get-tuple-element.91), custom_call_target="InvertDiagBlocksLowerTriangular" | custom-call | tf_op jit(solution)/shard_map/jit(cholesky)/cholesky | solution.py:72
  210.1 11.7 %cholesky.105 = f32[128,128]{1,0:T(8,128)S(1)} custom-call(f32[128,128]{1,0:T(8,128)S(1)} %convolution_subtract_fusion.1), custom_call_target="Cholesky" | custom-call | tf_op jit(solution)/shard_map/jit(cholesky)/cholesky | solution.py:72
  223.9 0.8 copy.25
  224.8 4.0 %while.1 = (s32[]{:T(128)}, f32[256,256]{1,0:T(8,128)S(1)}, s32[2,2]{1,0:T(2,128)S(1)}, f32[2,128,128]{2,1,0:T(8,128)S(1)}, s32[]{:T(128)}) while((s32[]{:T(128)}, f32[256,256]{1,0:T(8,128)S(1)}, s32[2,2]{1,0:T(2,128)S(1)}, f32[2,128,128]{2,1,0:T(8,128)S(1)}, s32[]{:T(128)}) %tuple.117), condition=%wide.while_cond, body=%wide.while_body.sunk | while | flops 2 | bytes 131189 | solution.py:73
  225.5 1.3 bitcast_dynamic-update-slice_fusion.2
  227.5 1.3 bitcast_dynamic-update-slice_fusion.2
  228.9 19.7 %custom-call.15 = f32[2,128,128]{1,2,0:T(8,128)S(1)} custom-call(f32[2,128,128]{2,1,0:T(8,128)S(1)} %get-tuple-element.11), custom_call_target="InvertDiagBlocksLowerTriangular" | custom-call | tf_op jit(solution)/shard_map/triangular_solve | solution.py:73
  248.5 1.1 fusion.2
  249.6 1.8 convolution_subtract_fusion
  251.4 1.1 fusion.110
  252.7 1.3 copy.29
  (193 shorter events, 14.9 us)
Async XLA Ops:
  7.2 14.1 %copy-start.9 = (f32[4,4,3,128]{3,1,2,0:T(4,128)S(1)}, f32[4,4,3,128]{3,1,2,0:T(4,128)}, u32[]{:S(2)}) copy-start(f32[4,4,3,128]{3,1,2,0:T(4,128)} %param.8) | copy-start | bytes 73732
  7.2 14.0 %copy-start.20 = (s32[4,4]{1,0:T(4,128)S(1)}, s32[4,4]{1,0:T(4,128)}, u32[]{:S(2)}) copy-start(s32[4,4]{1,0:T(4,128)} %param.10) | copy-start | bytes 196
  7.2 14.1 %copy-start = (s32[4,4,8]{2,1,0:T(4,128)S(1)}, s32[4,4,8]{2,1,0:T(4,128)}, u32[]{:S(2)}) copy-start(s32[4,4,8]{2,1,0:T(4,128)} %param.11) | copy-start | bytes 1540
  7.2 103.9 %all-reduce.4.cloned.1.call-start = ((), (), s32[]{:S(2)}) async-start(), calls=%async_computation | async-start | bytes 524288 | tf_op jit(solution)/shard_map/psum | solution.py:70
  8.0 18.1 %collective-permute-start = (bf16[1,4,3,128]{3,1,2,0:T(4,128)(2,1)S(1)}, bf16[1,4,3,128]{3,1,2,0:T(4,128)(2,1)S(1)}, u32[]{:S(2)}, u32[]{:S(2)}) collective-permute-start(bf16[1,4,3,128]{3,1,2,0:T(4,128)(2,1)S(1)} %get-tuple-element.121), channel_id=1, source_target_pairs={{0,4},{4,8},{8,12},{12,16},{16,20},{20,24},{24,28},{28,0},{1,5},{5... | collective-permute-start | bytes 9224 | tf_op jit(solution)/shard_map/ppermute | solution.py:15
  11.0 15.1 %collective-permute-start.1 = (bf16[1,4,3,128]{3,1,2,0:T(4,128)(2,1)S(1)}, bf16[1,4,3,128]{3,1,2,0:T(4,128)(2,1)S(1)}, u32[]{:S(2)}, u32[]{:S(2)}) collective-permute-start(bf16[1,4,3,128]{3,1,2,0:T(4,128)(2,1)S(1)} %get-tuple-element.122), channel_id=1, source_target_pairs={{4,0},{8,4},{12,8},{16,12},{20,16},{24,20},{28,24},{0,28},{5,1},{9... | collective-permute-start | bytes 9224 | tf_op jit(solution)/shard_map/ppermute | solution.py:16
  16.4 20.0 %collective-permute-start.4 = (bf16[1,4,128,256]{3,2,1,0:T(8,128)(2,1)S(1)}, bf16[1,4,128,256]{3,2,1,0:T(8,128)(2,1)S(1)}, u32[]{:S(2)}, u32[]{:S(2)}) collective-permute-start(bf16[1,4,128,256]{3,2,1,0:T(8,128)(2,1)S(1)} %get-tuple-element.84), channel_id=1, source_target_pairs={{0,4},{4,8},{8,12},{12,16},{16,20},{20,24},{24,28},{28,0},{1,5},{5... | collective-permute-start | bytes 786440 | tf_op jit(solution)/shard_map/ppermute | solution.py:15
  16.5 20.0 %collective-permute-start.5 = (bf16[1,4,128,256]{3,2,1,0:T(8,128)(2,1)S(1)}, bf16[1,4,128,256]{3,2,1,0:T(8,128)(2,1)S(1)}, u32[]{:S(2)}, u32[]{:S(2)}) collective-permute-start(bf16[1,4,128,256]{3,2,1,0:T(8,128)(2,1)S(1)} %get-tuple-element.85), channel_id=1, source_target_pairs={{4,0},{8,4},{12,8},{16,12},{20,16},{24,20},{28,24},{0,28},{5,1},{9... | collective-permute-start | bytes 786440 | tf_op jit(solution)/shard_map/ppermute | solution.py:16
  25.8 7.3 %copy-start.28 = (pred[16]{0:T(512)(128)(4,1)}, pred[16]{0:T(512)(128)(4,1)S(1)}, u32[]{:S(2)}) copy-start(pred[16]{0:T(512)(128)(4,1)S(1)} %get-tuple-element.50) | copy-start | bytes 52
  25.9 7.3 %copy-start.42 = (pred[16]{0:T(512)(128)(4,1)}, pred[16]{0:T(512)(128)(4,1)S(1)}, u32[]{:S(2)}) copy-start(pred[16]{0:T(512)(128)(4,1)S(1)} %get-tuple-element.123) | copy-start | bytes 52
  25.9 7.9 %copy-start.34 = (pred[16]{0:T(512)(128)(4,1)}, pred[16]{0:T(512)(128)(4,1)S(1)}, u32[]{:S(2)}) copy-start(pred[16]{0:T(512)(128)(4,1)S(1)} %get-tuple-element.131) | copy-start | bytes 52
  25.9 7.9 %copy-start.36 = (pred[16]{0:T(512)(128)(4,1)}, pred[16]{0:T(512)(128)(4,1)S(1)}, u32[]{:S(2)}) copy-start(pred[16]{0:T(512)(128)(4,1)S(1)} %get-tuple-element.129) | copy-start | bytes 52
  25.9 7.9 %copy-start.38 = (pred[16]{0:T(512)(128)(4,1)}, pred[16]{0:T(512)(128)(4,1)S(1)}, u32[]{:S(2)}) copy-start(pred[16]{0:T(512)(128)(4,1)S(1)} %get-tuple-element.127) | copy-start | bytes 52
  25.9 7.9 %copy-start.40 = (pred[16]{0:T(512)(128)(4,1)}, pred[16]{0:T(512)(128)(4,1)S(1)}, u32[]{:S(2)}) copy-start(pred[16]{0:T(512)(128)(4,1)S(1)} %get-tuple-element.125) | copy-start | bytes 52
  25.9 13.5 %copy-start.30 = (pred[16]{0:T(512)(128)(4,1)}, pred[16]{0:T(512)(128)(4,1)S(1)}, u32[]{:S(2)}) copy-start(pred[16]{0:T(512)(128)(4,1)S(1)} %get-tuple-element.133) | copy-start | bytes 52
  25.9 13.5 %copy-start.32 = (pred[16]{0:T(512)(128)(4,1)}, pred[16]{0:T(512)(128)(4,1)S(1)}, u32[]{:S(2)}) copy-start(pred[16]{0:T(512)(128)(4,1)S(1)} %get-tuple-element.135) | copy-start | bytes 52
  25.9 7.2 %copy-start.21 = (s32[1024]{0:T(1024)}, s32[1024]{0:T(1024)S(1)}, u32[]{:S(2)}) copy-start(s32[1024]{0:T(1024)S(1)} %pad_clamp_fusion.1) | copy-start | bytes 12292
  26.0 4.6 %copy-start.22 = (s32[1024]{0:T(1024)}, s32[1024]{0:T(1024)S(1)}, u32[]{:S(2)}) copy-start(s32[1024]{0:T(1024)S(1)} %pad_clamp_fusion.2) | copy-start | bytes 12292
  26.0 5.2 %copy-start.23 = (s32[1024]{0:T(1024)}, s32[1024]{0:T(1024)S(1)}, u32[]{:S(2)}) copy-start(s32[1024]{0:T(1024)S(1)} %pad_clamp_fusion.3) | copy-start | bytes 12292
  26.0 5.7 %copy-start.24 = (s32[1024]{0:T(1024)}, s32[1024]{0:T(1024)S(1)}, u32[]{:S(2)}) copy-start(s32[1024]{0:T(1024)S(1)} %pad_clamp_fusion.4) | copy-start | bytes 12292
  26.0 7.1 %copy-start.25 = (s32[1024]{0:T(1024)}, s32[1024]{0:T(1024)S(1)}, u32[]{:S(2)}) copy-start(s32[1024]{0:T(1024)S(1)} %pad_clamp_fusion.5) | copy-start | bytes 12292
  26.1 14.0 %copy-start.26 = (s32[1024]{0:T(1024)}, s32[1024]{0:T(1024)S(1)}, u32[]{:S(2)}) copy-start(s32[1024]{0:T(1024)S(1)} %pad_clamp_fusion.6) | copy-start | bytes 12292
  26.2 3.1 %collective-permute-start.2 = (bf16[6,1,3,128]{3,1,2,0:T(2,128)(2,1)S(1)}, bf16[6,1,3,128]{3,1,2,0:T(2,128)(2,1)S(1)}, u32[]{:S(2)}, u32[]{:S(2)}) collective-permute-start(bf16[6,1,3,128]{3,1,2,0:T(2,128)(2,1)S(1)} %get-tuple-element.119), channel_id=1, source_target_pairs={{0,1},{1,2},{2,3},{3,0},{4,5},{5,6},{6,7},{7,4},{8,9},{9,10},{10,1... | collective-permute-start | bytes 13832 | tf_op jit(solution)/shard_map/ppermute | solution.py:15
  26.2 3.1 %collective-permute-start.3 = (bf16[6,1,3,128]{3,1,2,0:T(2,128)(2,1)S(1)}, bf16[6,1,3,128]{3,1,2,0:T(2,128)(2,1)S(1)}, u32[]{:S(2)}, u32[]{:S(2)}) collective-permute-start(bf16[6,1,3,128]{3,1,2,0:T(2,128)(2,1)S(1)} %get-tuple-element.120), channel_id=1, source_target_pairs={{1,0},{2,1},{3,2},{0,3},{5,4},{6,5},{7,6},{4,7},{9,8},{10,9},{11,1... | collective-permute-start | bytes 13832 | tf_op jit(solution)/shard_map/ppermute | solution.py:16
  28.0 18.0 %copy-start.27 = (s32[1024]{0:T(1024)}, s32[1024]{0:T(1024)S(1)}, u32[]{:S(2)}) copy-start(s32[1024]{0:T(1024)S(1)} %pad_clamp_fusion.7) | copy-start | bytes 12292
  36.4 9.6 %copy-start.1 = (bf16[1,4,128,256]{3,2,1,0:T(8,128)(2,1)}, bf16[1,4,128,256]{3,2,1,0:T(8,128)(2,1)S(1)}, u32[]{:S(2)}) copy-start(bf16[1,4,128,256]{3,2,1,0:T(8,128)(2,1)S(1)} %collective-permute-done.4) | copy-start | bytes 786436
  36.5 9.5 %copy-start.2 = (bf16[1,4,128,256]{3,2,1,0:T(8,128)(2,1)}, bf16[1,4,128,256]{3,2,1,0:T(8,128)(2,1)S(1)}, u32[]{:S(2)}) copy-start(bf16[1,4,128,256]{3,2,1,0:T(8,128)(2,1)S(1)} %collective-permute-done.5) | copy-start | bytes 786436
  36.6 9.4 %collective-permute-start.6 = (bf16[6,1,128,256]{3,2,1,0:T(8,128)(2,1)S(1)}, bf16[6,1,128,256]{3,2,1,0:T(8,128)(2,1)S(1)}, u32[]{:S(2)}, u32[]{:S(2)}) collective-permute-start(bf16[6,1,128,256]{3,2,1,0:T(8,128)(2,1)S(1)} %get-tuple-element.82), channel_id=1, source_target_pairs={{0,1},{1,2},{2,3},{3,0},{4,5},{5,6},{6,7},{7,4},{8,9},{9,10},{10,1... | collective-permute-start | bytes 1179656 | tf_op jit(solution)/shard_map/ppermute | solution.py:15
  38.3 8.9 %collective-permute-start.7 = (bf16[6,1,128,256]{3,2,1,0:T(8,128)(2,1)S(1)}, bf16[6,1,128,256]{3,2,1,0:T(8,128)(2,1)S(1)}, u32[]{:S(2)}, u32[]{:S(2)}) collective-permute-start(bf16[6,1,128,256]{3,2,1,0:T(8,128)(2,1)S(1)} %get-tuple-element.83), channel_id=1, source_target_pairs={{1,0},{2,1},{3,2},{0,3},{5,4},{6,5},{7,6},{4,7},{9,8},{10,9},{11,1... | collective-permute-start | bytes 1179656 | tf_op jit(solution)/shard_map/ppermute | solution.py:16
  57.8 3.6 %copy-start.43 = (pred[16]{0:T(512)(128)(4,1)S(1)}, pred[16]{0:T(512)(128)(4,1)}, u32[]{:S(2)}) copy-start(pred[16]{0:T(512)(128)(4,1)} %copy-done.42) | copy-start | bytes 52
  61.4 2.4 copy-start.8
  61.4 2.4 copy-start.41
  67.3 1.8 copy-start.5
  67.3 1.8 copy-start.11
  67.3 1.8 copy-start.12
  67.3 1.8 copy-start.13
  67.4 1.8 copy-start.35
  69.1 1.8 copy-start.4
  69.1 1.8 copy-start.17
  69.1 1.8 copy-start.18
  69.1 1.8 copy-start.19
  69.2 1.8 copy-start.33
  70.9 1.8 copy-start.3
  70.9 1.8 copy-start.14
  70.9 1.8 copy-start.15
  70.9 1.8 copy-start.16
  71.0 1.8 copy-start.31
  81.2 104.1 %all-reduce.6.cloned.1.call-start = ((), (), s32[]{:S(2)}) async-start(), calls=%async_computation.1 | async-start | bytes 524288 | tf_op jit(solution)/shard_map/psum | solution.py:71
  (6 other events, 10.4 us)
Sparse Core Ops, SparseCore 0:
  81.3 29.6 all-reduce.3
  114.8 70.5 all-reduce.5
